TPU v7x, 512 devices: a whole 4x8x8 slice. The times are simulated.
512 devices in a mesh: dp: 16 (over x, z_lo, core), fsdp: 32 (over y, z_hi).
Axes of the slice: x: 4, y: 8, z: 8 (z_hi: 4, z_lo: 2; z = z_hi * 2 + z_lo), core: 2. Of those that a mesh axis runs over, the one named last changes fastest.
Arguments:
- tokens: bfloat16 [2048, 4096], P(('dp', 'fsdp')), may hold values from -6 to 6
- cotangent: bfloat16 [2048, 4096], P(('dp', 'fsdp')), may hold values from -6 to 6
- w_in: bfloat16 [1152, 128, 128], P('fsdp'), may hold values from -0.1875 to 0.1875
- w_out: bfloat16 [1152, 128, 128], P('fsdp'), may hold values from -0.09375 to 0.09375
- in_rows: int32 [1152], P('fsdp'), may hold values from -1 to 127, as said below
- in_cols: int32 [1152], P('fsdp'), may hold values from -1 to 31, as said below
- out_rows: int32 [1152], P('fsdp'), may hold values from -1 to 127, as said below
- out_cols: int32 [1152], P('fsdp'), may hold values from -1 to 31, as said below
Outputs:
- mixed: bfloat16 [2048, 4096], P(('dp', 'fsdp'))
- input_grad: bfloat16 [2048, 4096], P(('dp', 'fsdp'))
- in_grad: bfloat16 [1152, 128, 128], P('fsdp')
- out_grad: bfloat16 [1152, 128, 128], P('fsdp')
Inputs may be any that keep to these rules, and one draw needn't show every extreme that they name: `in_rows`: slot s lies on fsdp device s // 36. A live slot names a hidden panel r with r // 4 equal to that device; -1 marks an empty slot, and empty slots follow the live ones of their device. No (panel, column block) pair is named twice. On some device all 36 slots are live, on every device at least 24. `in_cols`: -1 exactly where in_rows is -1. `out_rows`: as in_rows, for w_out. `out_cols`: -1 exactly where out_rows is -1.
All inputs are finite; a program needn't handle non-finite values.
Results may differ from a plain program's by a relative error of at most 0.025.
Values may be sent and summed in bfloat16 or wider, within the bound.
A program may use at most 64 MiB of HBM per device.

v0:
```python
import jax
import jax.numpy as jnp
from jax import lax
from jax.sharding import PartitionSpec as P

FF = 16384


def gelu_slope(values):
    cdf = 0.5 * (1.0 + jax.scipy.special.erf(values * 0.7071067811865476))
    return cdf + values * jnp.exp(-0.5 * values * values) * 0.3989422804014327


def slot_tables(slot_rows, slot_cols, per_dev):
    is_live = slot_rows >= 0
    safe_panel = jnp.where(is_live, slot_rows % per_dev, 0)
    safe_column = jnp.where(is_live, slot_cols, 0)
    return (is_live, safe_panel, safe_column)


def pick_blocks(values, slot_index, group_count):
    shaped = values.reshape(values.shape[0], group_count, 128)
    return jnp.take(shaped, slot_index, axis=1)


def fold_slots(is_live, target, contrib, count):
    selector = jnp.logical_and(
        target[:, None] == jnp.arange(count, dtype=jnp.int32)[None, :], is_live[:, None]
    )
    selector = selector.astype(jnp.float32)
    summed = jnp.einsum("stf,sp->tpf", contrib, selector, precision=lax.Precision.HIGHEST)
    return summed.reshape(summed.shape[0], -1)


def local(tokens, cotangent, w_in, w_out, in_rows, in_cols, out_rows, out_cols):
    nfsdp = lax.axis_size("fsdp")
    per_dev = FF // 128 // nfsdp
    width = tokens.shape[1]
    ncol = width // 128
    in_live, in_panel, in_column = slot_tables(in_rows, in_cols, per_dev)
    out_live, out_panel, out_column = slot_tables(out_rows, out_cols, per_dev)
    gathered = lax.all_gather(tokens, "fsdp", axis=0, tiled=True)
    x_pick = pick_blocks(gathered, in_column, ncol)
    pre_act = fold_slots(
        in_live,
        in_panel,
        jnp.einsum("tsd,sfd->stf", x_pick, w_in, preferred_element_type=jnp.float32),
        per_dev,
    )
    hidden = jax.nn.gelu(pre_act, approximate=False).astype(jnp.bfloat16)
    h_pick = pick_blocks(hidden, out_panel, per_dev)
    row_part = h_pick
    contrib = jnp.einsum("tsf,sfd->std", row_part, w_out, preferred_element_type=jnp.float32)
    mixed = lax.psum_scatter(
        fold_slots(out_live, out_column, contrib, ncol).astype(jnp.bfloat16),
        "fsdp",
        scatter_dimension=0,
        tiled=True,
    )
    cot_rows = lax.all_gather(cotangent, "fsdp", axis=0, tiled=True)
    c_pick = pick_blocks(cot_rows, out_column, ncol)
    d_hidden = fold_slots(
        out_live,
        out_panel,
        jnp.einsum("tsd,sfd->stf", c_pick, w_out, preferred_element_type=jnp.float32),
        per_dev,
    )
    d_pre = (d_hidden * gelu_slope(pre_act)).astype(jnp.bfloat16)
    d_pick = pick_blocks(d_pre, in_panel, per_dev)
    grad_out = jnp.einsum("tsf,tsd->sfd", h_pick, c_pick, preferred_element_type=jnp.float32)
    grad_out = jnp.where(out_live[:, None, None], grad_out, 0.0)
    row_part = d_pick
    contrib = jnp.einsum("tsf,sfd->std", row_part, w_in, preferred_element_type=jnp.float32)
    input_grad = lax.psum_scatter(
        fold_slots(in_live, in_column, contrib, ncol).astype(jnp.bfloat16),
        "fsdp",
        scatter_dimension=0,
        tiled=True,
    )
    grad_in = jnp.einsum("tsf,tsd->sfd", d_pick, x_pick, preferred_element_type=jnp.float32)
    grad_in = jnp.where(in_live[:, None, None], grad_in, 0.0)
    out_total, in_total = (
        lax.psum(grad_out.astype(jnp.bfloat16), "dp").astype(jnp.float32),
        lax.psum(grad_in.astype(jnp.bfloat16), "dp").astype(jnp.float32),
    )
    return (mixed, input_grad, in_total.astype(jnp.bfloat16), out_total.astype(jnp.bfloat16))


def solution(mesh):
    placed = (
        P(("dp", "fsdp"), None),
        P(("dp", "fsdp"), None),
        P("fsdp", None, None),
        P("fsdp", None, None),
        P("fsdp"),
        P("fsdp"),
        P("fsdp"),
        P("fsdp"),
    )
    return jax.shard_map(
        local,
        mesh=mesh,
        in_specs=placed,
        out_specs=(
            P(("dp", "fsdp"), None),
            P(("dp", "fsdp"), None),
            P("fsdp", None, None),
            P("fsdp", None, None),
        ),
        check_vma=False,
    )
```

profile of v0, /device:TPU:8, one launch (start us, length us, event | category | flops | bytes accessed | tf_op | source)
XLA Modules:
  0.0 687.5 jit_solution(2108964944030363270)
XLA Ops:
  10.2 88.5 %all-gather.5.cloned.1.call-done = bf16[32,4,4096]{2,1,0:T(4,128)(2,1)} async-done(((bf16[1,4,4096]{2,1,0:T(4,128)(2,1)}), bf16[32,4,4096]{2,1,0:T(4,128)(2,1)}) %all-gather.5.cloned.1.call-update) | async-done | bytes 1048592 | tf_op jit(solution)/shard_map/all_gather | solution.py:42
  98.8 2.1 reshape.40
  101.3 81.3 %all-gather.7.cloned.1.call-done = bf16[32,4,4096]{2,1,0:T(4,128)(2,1)} async-done(((bf16[1,4,4096]{2,1,0:T(4,128)(2,1)}), bf16[32,4,4096]{2,1,0:T(4,128)(2,1)}) %all-gather.7.cloned.1.call-update) | async-done | bytes 1048592 | tf_op jit(solution)/shard_map/all_gather | solution.py:60
  182.6 2.9 reshape.41
  185.5 1.6 copy.42
  187.2 1.8 gather_fusion
  189.0 2.3 fusion.24
  191.2 3.0 fusion.6
  195.0 2.3 fusion.18
  197.2 2.3 fusion.2
  200.2 1.8 gather_fusion.3
  202.0 1.8 fusion.15
  203.8 2.8 fusion.11
  206.6 1.4 copy.69
  208.0 1.8 gather_fusion.1
  209.8 2.3 fusion.21
  212.2 2.8 fusion.8
  215.0 1.5 copy.70
  217.7 3.2 select_convert_fusion.1
  220.9 1.8 select_convert_fusion
  224.6 313.1 %all-reduce.7.cloned.1.call-done = (bf16[128,4096]{1,0:T(8,128)(2,1)}, bf16[128,4096]{1,0:T(8,128)(2,1)}) async-done(((bf16[128,4096]{1,0:T(8,128)(2,1)}, bf16[128,4096]{1,0:T(8,128)(2,1)}), (bf16[128,4096]{1,0:T(8,128)(2,1)}, bf16[128,4096]{1,0:T(8,128)(2,1)})) %all-reduce.7.cloned.1.call-update) | async-done | bytes 2097168
  537.7 1.5 constant_dynamic-slice_fusion
  539.3 138.2 %all-reduce.9.cloned.1.call-done = (bf16[36,128,128]{2,1,0:T(8,128)(2,1)}, bf16[36,128,128]{2,1,0:T(8,128)(2,1)}) async-done(((bf16[36,128,128]{2,1,0:T(8,128)(2,1)}, bf16[36,128,128]{2,1,0:T(8,128)(2,1)}), (bf16[36,128,128]{2,1,0:T(8,128)(2,1)}, bf16[36,128,128]{2,1,0:T(8,128)(2,1)})) %all-reduce.9.cloned.1.call-update) | async-done | bytes 2359312 | tf_op jit(solution)/shard_map/psum | solution.py:84
  677.4 2.5 copy.75
  (41 shorter events, 8.4 us)
Async XLA Ops:
  7.2 181.8 %copy-start = (bf16[36,128,128]{2,1,0:T(8,128)(2,1)S(1)}, bf16[36,128,128]{2,1,0:T(8,128)(2,1)}, u32[]{:S(2)}) copy-start(bf16[36,128,128]{2,1,0:T(8,128)(2,1)} %param.14) | copy-start | bytes 3538948
  7.2 91.6 %all-gather.5.cloned.1.call-start = ((), (), s32[]{:S(2)}) async-start(), calls=%async_computation | async-start | bytes 1081344 | tf_op jit(solution)/shard_map/all_gather | solution.py:42
  7.9 174.7 %all-gather.7.cloned.1.call-start = ((), (), s32[]{:S(2)}) async-start(), calls=%async_computation.1 | async-start | bytes 1081344 | tf_op jit(solution)/shard_map/all_gather | solution.py:60
  8.7 529.1 %all-reduce.7.cloned.1.call-start = ((), (), s32[]{:S(2)}) async-start(), calls=%async_computation.2 | async-start | bytes 4194304
  10.1 184.9 %copy-start.5 = (pred[36]{0:T(512)(128)(4,1)}, pred[36]{0:T(512)(128)(4,1)S(1)}, u32[]{:S(2)}) copy-start(pred[36]{0:T(512)(128)(4,1)S(1)} %get-tuple-element.12) | copy-start | bytes 112
  10.1 199.7 %copy-start.7 = (pred[36]{0:T(512)(128)(4,1)}, pred[36]{0:T(512)(128)(4,1)S(1)}, u32[]{:S(2)}) copy-start(pred[36]{0:T(512)(128)(4,1)S(1)} %get-tuple-element.21) | copy-start | bytes 112
  197.2 2.3 copy-start.4
  216.4 1.3 copy-start.1
  216.5 461.0 %all-reduce.9.cloned.1.call-start = ((), (), s32[]{:S(2)}) async-start(), calls=%async_computation.3 | async-start | bytes 4718592 | tf_op jit(solution)/shard_map/psum | solution.py:84
  217.7 3.2 copy-start.2
  217.7 3.2 copy-start.6
  217.7 3.2 copy-start.8
  677.4 2.5 copy-start.3
Sparse Core Ops, SparseCore 0:
  11.2 87.5 all-gather.4
  101.9 80.6 all-gather.6
  216.6 321.1 all-reduce.6
  541.4 135.9 all-reduce.8
where the time goes:
time: 688 us; the launch traced here: 687 us
  waiting for transfers between devices  622 us (90%)
  matrix products  24.4 us (4%)
  local copies, waits for them, and re-layouts  23.8 us (3%)
  between operations  14.6 us (2%)
    unnamed x5, waiting for transfers between devices  315 us
    psum x1, waiting for transfers between devices, local(): lax.psum(grad_in.astype(jnp.bfloat16), 'dp').astype(jnp.float32)  138 us
    all_gather x1, waiting for transfers between devices, local(): gathered = lax.all_gather(tokens, 'fsdp', axis=0, tiled=True)  88.5 us
    all_gather x1, waiting for transfers between devices, local(): cot_rows = lax.all_gather(cotangent, 'fsdp', axis=0, tiled=True)  81.3 us
  transfers between devices with their start and end apart: 4, of which 4 were waited for; matrix products, arithmetic and copies ran while one was open for 2% of the time, Pallas kernels for 0%

commit v1 on v0

--- a/solution.py
+++ b/solution.py
@@ -81,7 +81,7 @@
     grad_in = jnp.where(in_live[:, None, None], grad_in, 0.0)
     out_total, in_total = (
         lax.psum(grad_out.astype(jnp.bfloat16), "dp").astype(jnp.float32),
-        lax.psum(grad_in.astype(jnp.bfloat16), "dp").astype(jnp.float32),
+        jnp.sum(lax.all_gather(grad_in.astype(jnp.bfloat16), "dp"), axis=0).astype(jnp.float32),
     )
     return (mixed, input_grad, in_total.astype(jnp.bfloat16), out_total.astype(jnp.bfloat16))
 

time: 688 us -> 791 us (1.15)
  the two profiles are of different devices: /device:TPU:8 before, /device:TPU:1 now
where the time goes in v1:
time: 791 us; the launch traced here: 790 us
  waiting for transfers between devices  714 us (90%)
  matrix products  24.3 us (3%)
  local copies, waits for them, and re-layouts  23.9 us (3%)
  between operations  14.6 us (2%)
  other arithmetic  13.7 us (2%)
    unnamed x6, waiting for transfers between devices  299 us
    all_gather x1, waiting for transfers between devices, local(): lax.all_gather(grad_in.astype(jnp.bfloat16), 'dp')  125 us
    psum x1, waiting for transfers between devices, local(): lax.psum(grad_out.astype(jnp.bfloat16), 'dp').astype(jnp.float32)  122 us
    all_gather x1, waiting for transfers between devices, local(): gathered = lax.all_gather(tokens, 'fsdp', axis=0, tiled=True)  86.8 us
    all_gather x1, waiting for transfers between devices, local(): cot_rows = lax.all_gather(cotangent, 'fsdp', axis=0, tiled=True)  81.3 us
  transfers between devices with their start and end apart: 5, of which 5 were waited for; matrix products, arithmetic and copies ran while one was open for 3% of the time, Pallas kernels for 0%

profile of v1, /device:TPU:1, one launch (start us, length us, event | category | flops | bytes accessed | tf_op | source)
XLA Modules:
  0.0 790.5 jit_solution(13625742948913544367)
XLA Ops:
  10.2 86.8 %all-gather.9.cloned.1.call-done = bf16[32,4,4096]{2,1,0:T(4,128)(2,1)} async-done(((bf16[1,4,4096]{2,1,0:T(4,128)(2,1)}), bf16[32,4,4096]{2,1,0:T(4,128)(2,1)}) %all-gather.9.cloned.1.call-update) | async-done | bytes 1048592 | tf_op jit(solution)/shard_map/all_gather | solution.py:42
  97.0 2.1 reshape.40
  99.6 81.3 %all-gather.11.cloned.1.call-done = bf16[32,4,4096]{2,1,0:T(4,128)(2,1)} async-done(((bf16[1,4,4096]{2,1,0:T(4,128)(2,1)}), bf16[32,4,4096]{2,1,0:T(4,128)(2,1)}) %all-gather.11.cloned.1.call-update) | async-done | bytes 1048592 | tf_op jit(solution)/shard_map/all_gather | solution.py:60
  180.9 2.9 reshape.41
  183.8 1.6 copy.42
  185.5 1.8 gather_fusion
  187.3 2.3 fusion.24
  189.5 3.0 fusion.6
  193.3 2.3 fusion.18
  195.5 2.3 fusion.2
  198.5 1.8 gather_fusion.3
  200.3 1.8 fusion.15
  202.1 2.8 fusion.11
  206.4 1.8 gather_fusion.1
  208.2 2.3 fusion.21
  210.6 2.8 fusion.8
  216.0 3.1 select_convert_fusion.1
  220.4 1.8 select_convert_fusion
  224.1 297.3 %all-reduce.8.cloned.1.call-done = (bf16[128,4096]{1,0:T(8,128)(2,1)}, bf16[128,4096]{1,0:T(8,128)(2,1)}) async-done(((bf16[128,4096]{1,0:T(8,128)(2,1)}, bf16[128,4096]{1,0:T(8,128)(2,1)}), (bf16[128,4096]{1,0:T(8,128)(2,1)}, bf16[128,4096]{1,0:T(8,128)(2,1)})) %all-reduce.8.cloned.1.call-update) | async-done | bytes 2097168
  521.4 1.5 constant_dynamic-slice_fusion
  522.9 124.7 %all-gather.7.cloned.1.call-done = bf16[576,128,128]{2,1,0:T(8,128)(2,1)} async-done(((bf16[36,128,128]{2,1,0:T(8,128)(2,1)}), bf16[576,128,128]{2,1,0:T(8,128)(2,1)}) %all-gather.7.cloned.1.call-update) | async-done | bytes 18874384 | tf_op jit(solution)/shard_map/all_gather | solution.py:84
  647.6 11.6 %reduce_sum.12 = bf16[36,128,128]{2,1,0:T(8,128)(2,1)} reduce(bf16[16,36,128,128]{3,2,1,0:T(8,128)(2,1)} %bitcast.99, bf16[]{:T(256)} %constant.108.clone.1), dimensions={0}, to_apply=%region_2.5 | reduce | flops 8847360 | bytes 20054018 | tf_op jit(solution)/shard_map/reduce_sum | solution.py:84
  659.2 122.3 %all-reduce.6.cloned.1.call-done = bf16[36,128,128]{2,1,0:T(8,128)(2,1)} async-done(((bf16[36,128,128]{2,1,0:T(8,128)(2,1)}), bf16[36,128,128]{2,1,0:T(8,128)(2,1)}) %all-reduce.6.cloned.1.call-update) | async-done | bytes 1179664 | tf_op jit(solution)/shard_map/psum | solution.py:83
  781.5 2.4 copy.74
  (38 shorter events, 11.5 us)
Async XLA Ops:
  7.2 180.1 %copy-start = (bf16[36,128,128]{2,1,0:T(8,128)(2,1)S(1)}, bf16[36,128,128]{2,1,0:T(8,128)(2,1)}, u32[]{:S(2)}) copy-start(bf16[36,128,128]{2,1,0:T(8,128)(2,1)} %param.14) | copy-start | bytes 3538948
  7.2 89.9 %all-gather.9.cloned.1.call-start = ((), (), s32[]{:S(2)}) async-start(), calls=%async_computation.2 | async-start | bytes 1081344 | tf_op jit(solution)/shard_map/all_gather | solution.py:42
  7.9 173.0 %all-gather.11.cloned.1.call-start = ((), (), s32[]{:S(2)}) async-start(), calls=%async_computation.3 | async-start | bytes 1081344 | tf_op jit(solution)/shard_map/all_gather | solution.py:60
  8.7 512.7 %all-reduce.8.cloned.1.call-start = ((), (), s32[]{:S(2)}) async-start(), calls=%async_computation.4 | async-start | bytes 4194304
  9.4 177.9 %copy-start.5 = (pred[36]{0:T(512)(128)(4,1)}, pred[36]{0:T(512)(128)(4,1)S(1)}, u32[]{:S(2)}) copy-start(pred[36]{0:T(512)(128)(4,1)S(1)} %get-tuple-element.23) | copy-start | bytes 112
  9.4 190.9 %copy-start.4 = (pred[36]{0:T(512)(128)(4,1)}, pred[36]{0:T(512)(128)(4,1)S(1)}, u32[]{:S(2)}) copy-start(pred[36]{0:T(512)(128)(4,1)S(1)} %get-tuple-element.8) | copy-start | bytes 112
  195.5 2.3 copy-start.3
  214.7 1.3 copy-start.1
  214.8 432.9 %all-gather.7.cloned.1.call-start = ((), (), s32[]{:S(2)}) async-start(), calls=%async_computation.1 | async-start | bytes 20054016 | tf_op jit(solution)/shard_map/all_gather | solution.py:84
  219.1 1.3 copy-start.2
  219.1 562.4 %all-reduce.6.cloned.1.call-start = ((), (), s32[]{:S(2)}) async-start(), calls=%async_computation | async-start | bytes 2359296 | tf_op jit(solution)/shard_map/psum | solution.py:83
Sparse Core Ops, SparseCore 0:
  11.2 85.8 all-gather.8
  100.2 80.6 all-gather.10
  214.9 306.4 all-reduce.7
  524.2 123.3 all-gather.6
  650.7 130.8 all-reduce.5
